TPU v7x, 256 devices: a whole 4x4x8 slice. The times are simulated.
256 devices in a mesh: cls: 4 (over z_hi), grp: 4 (over x), dom: 16 (over y, z_lo, core).
Axes of the slice: x: 4, y: 4, z: 8 (z_hi: 4, z_lo: 2; z = z_hi * 2 + z_lo), core: 2. Of those that a mesh axis runs over, the one named last changes fastest.
Arguments:
- particle_images: bfloat16 [2560, 8192], P(('grp', 'dom')), may hold values from -110 to 110, as said below
- particle_groups: int32 [2560], P(('grp', 'dom')), may hold values from 0 to 7
- live_counts: int32 [64], P(('grp', 'dom')), may hold values from 1 to 40, as said below
- ctf_table: float32 [8, 4096], replicated, may hold values from -1 to 1
- projections: bfloat16 [8192, 8, 200], P(('grp', 'dom'), 'cls'), may hold values from -0.25 to 0.25
Outputs:
- insertions: float32 [8, 200, 8192], P('cls', None, ('grp', 'dom'))
- class_weights: float32 [8, 8, 200], P('cls')
- log_evidence: float32 [2560], P(('grp', 'dom'))
Inputs may be any that keep to these rules, and one draw needn't show every extreme that they name: `particle_images`: particle image coefficients. `live_counts`: live particles of one shard; in every draw some shard has all 40 slots live.
All inputs are finite; a program needn't handle non-finite values.
Results may differ from a plain program's by a relative error of at most 0.012.
The roundings to bfloat16 on the way count: a program that leaves them out, or rounds other values in their place, can miss the bound.
Values may be sent and summed in bfloat16 or wider, within the bound.
No kernel may reach another device: no remote copies, remote signals or barrier semaphores. Data moves between devices by JAX's collectives and lax.ppermute only.
A program may use at most 128 MiB of HBM per device.

v0:
```python
import math

import jax
import jax.numpy as jnp
from jax import lax
from jax.sharding import PartitionSpec as P

IMG = 64
SIDE = 5
GROUPS = 8


def joined(array, axis, combine):
    everything = jax.tree.map(lambda part: lax.all_gather(part, axis), array)
    first = jax.tree.map(lambda part: part[0], everything)

    def turn(k, so_far):
        return combine(so_far, jax.tree.map(lambda part: part[k], everything))

    return lax.fori_loop(1, lax.axis_size(axis), turn, first)


def build_shifted(images, groups, ctf_table):
    freqs = IMG * IMG
    index = jnp.arange(freqs, dtype=jnp.int32)
    rowf = index // IMG
    colf = index % IMG
    shift_index = jnp.arange(SIDE * SIDE, dtype=jnp.int32)
    offx = shift_index // SIDE - SIDE // 2
    offy = shift_index % SIDE - SIDE // 2
    phase = (offx[:, None] * rowf[None, :] + offy[:, None] * colf[None, :]) % IMG
    theta = phase.astype(jnp.float32) * (2.0 * math.pi / IMG)
    cosv = jnp.cos(theta)[None]
    sinv = jnp.sin(theta)[None]
    onehot = (groups[:, None] == jnp.arange(GROUPS, dtype=jnp.int32)[None, :]).astype(jnp.float32)
    ctf_rows = jnp.dot(onehot, ctf_table, precision=lax.Precision.HIGHEST)[:, None, :]
    real = images[:, :freqs].astype(jnp.float32)[:, None, :]
    imag = images[:, freqs:].astype(jnp.float32)[:, None, :]
    shifted_real = ctf_rows * (real * cosv + imag * sinv)
    shifted_imag = ctf_rows * (imag * cosv - real * sinv)
    shifted = jnp.concatenate([shifted_real, shifted_imag], axis=2).astype(jnp.bfloat16)
    return (shifted.reshape(images.shape[0] * SIDE * SIDE, 2 * freqs), onehot)


def combine_totals(first, second):
    top = jnp.maximum(first[0], second[0])
    total = first[1] * jnp.exp(first[0] - top) + second[1] * jnp.exp(second[0] - top)
    return (top, total)


def body(particle_images, particle_groups, live_counts, ctf_table, projections):
    npart = particle_images.shape[0]
    shifts = SIDE * SIDE
    kdev = projections.shape[1]
    nrot = projections.shape[2]
    width = kdev * nrot
    shifted, onehot = build_shifted(particle_images, particle_groups, ctf_table)
    ctf_square = jnp.concatenate([ctf_table, ctf_table], axis=1) ** 2
    piece = lax.all_gather(projections, ("grp", "dom"), axis=0, tiled=True)
    rows = piece.shape[0]
    flat = piece.reshape(rows, width)
    squares = flat.astype(jnp.float32) ** 2
    scores = jnp.dot(shifted, flat, preferred_element_type=jnp.float32)
    power = jnp.dot(ctf_square, squares, precision=lax.Precision.HIGHEST)
    scores, power = (scores, power)
    power_rows = jnp.dot(onehot, power, precision=lax.Precision.HIGHEST)
    loglik = scores.reshape(npart, shifts, width) - 0.5 * power_rows[:, None, :]
    local_top = jnp.max(loglik, axis=(1, 2))
    local_total = jnp.sum(jnp.exp(loglik - local_top[:, None, None]), axis=(1, 2))
    top, total = joined((local_top, local_total), "cls", combine_totals)
    live = jnp.arange(npart, dtype=jnp.int32) < live_counts[0]
    posterior = jnp.exp(loglik - top[:, None, None]) / total[:, None, None]
    posterior = jnp.where(live[:, None, None], posterior, jnp.float32(0.0))
    evidence = jnp.where(live, top + jnp.log(total), jnp.float32(0.0))
    low = posterior.astype(jnp.bfloat16).reshape(npart * shifts, width)
    sums = lax.dot_general(
        low, shifted, (((0,), (0,)), ((), ())), preferred_element_type=jnp.float32
    )
    sums = sums.reshape(kdev, nrot, shifted.shape[1])
    insertions = lax.psum_scatter(sums, ("grp", "dom"), scatter_dimension=2, tiled=True)
    local_weights = jnp.dot(onehot.T, jnp.sum(posterior, axis=1), precision=lax.Precision.HIGHEST)
    local_weights = jnp.transpose(local_weights.reshape(GROUPS, kdev, nrot), (1, 0, 2))
    class_weights = lax.psum(local_weights, ("grp", "dom"))
    return (insertions, class_weights, evidence)


def solution(mesh):
    placed = (
        P(("grp", "dom"), None),
        P(("grp", "dom")),
        P(("grp", "dom")),
        P(),
        P(("grp", "dom"), "cls", None),
    )
    return jax.shard_map(
        body,
        mesh=mesh,
        in_specs=placed,
        out_specs=(P("cls", None, ("grp", "dom")), P("cls", None, None), P(("grp", "dom"))),
        check_vma=False,
    )
```

profile of v0, /device:TPU:32, one launch (start us, length us, event | category | flops | bytes accessed | tf_op | source)
XLA Modules:
  0.0 506.0 jit_solution(8033443848924879521)
XLA Ops:
  7.2 0.7 all-gather.4.cloned.1.call-update
  7.9 0.0 reduce-scatter.2.cloned.1.call-start
  8.6 1.4 fusion.28
  10.0 2.1 fusion.16
  12.2 1.2 slice_convert_fusion.1
  13.3 8.3 %multiply_convert_fusion.1 = (bf16[40,25,4096]{2,0,1:T(8,128)(2,1)}, bf16[40,25,4096]{2,0,1:T(8,128)(2,1)}) fusion(f32[25,4096]{1,0:T(8,128)S(1)} %get-tuple-element.159, f32[40,4096]{1,0:T(8,128)S(1)} %get-tuple-element.157, f32[25,4096]{1,0:T(8,128)S(1)} %get-tuple-element.158, f32[40,4096]{1,0:T(8,128)S(1)} %get-tuple-element.156, f32[40,4096]{1,0:T(8,128)S(1)} %fusion.28), kind=kLoop, calls=%fused_computation.15 | loop fusion | flops 40960000 | bytes 19169280 | tf_op jit(solution)/shard_map/convert.4
  21.6 12.1 %copy.15 = bf16[40,25,4096]{2,1,0:T(8,128)(2,1)} copy(bf16[40,25,4096]{2,0,1:T(8,128)(2,1)} %get-tuple-element.154) | data formatting | bytes 16384000 | tf_op jit(solution)/shard_map/convert.4
  33.8 10.0 %mul.221 = bf16[1000,4096]{1,0:T(8,128)(2,1)} reshape(bf16[40,25,4096]{2,1,0:T(8,128)(2,1)} %copy.15) | data formatting | bytes 16384000 | tf_op jit(solution)/shard_map/mul | solution.py:39
  43.8 12.1 %copy.16 = bf16[40,25,4096]{2,1,0:T(8,128)(2,1)} copy(bf16[40,25,4096]{2,0,1:T(8,128)(2,1)} %get-tuple-element.155) | data formatting | bytes 16384000 | tf_op jit(solution)/shard_map/convert.5
  55.9 10.3 %mul.222 = bf16[1000,4096]{1,0:T(8,128)(2,1)} reshape(bf16[40,25,4096]{2,1,0:T(8,128)(2,1)} %copy.16) | data formatting | bytes 16384000 | tf_op jit(solution)/shard_map/mul | solution.py:40
  66.2 0.6 dynamic-slice
  67.4 69.2 %all-gather.4.cloned.1.call-done = bf16[8192,2,200]{0,2,1:T(8,128)(2,1)} async-done(((bf16[128,2,200]{0,2,1:T(8,128)(2,1)}), bf16[8192,2,200]{0,2,1:T(8,128)(2,1)}) %all-gather.4.cloned.1.call-update) | async-done | bytes 6553616 | tf_op jit(solution)/shard_map/all_gather | solution.py:59
  136.7 12.6 %fusion.9 = f32[8,400]{1,0:T(8,128)S(1)} fusion(bf16[8192,400]{0,1:T(8,128)(2,1)} %bitcast.38, f32[8,4096]{1,0:T(8,128)S(1)} %copy-done), kind=kOutput, calls=%fused_computation.16 | convolution fusion | flops 321257472 | bytes 6697472 | tf_op jit(solution)/shard_map/dot_general | solution.py:64
  149.3 0.2 convolution_multiply_fusion
  149.5 14.6 %subtract_reduce_fusion = (f32[40]{0:T(128)S(1)}, f32[40,25,400]{2,0,1:T(8,128)S(1)}) fusion(f32[40,400]{1,0:T(8,128)S(1)} %convolution_multiply_fusion, bf16[8192,400,1]{0,1,2:T(8,128)(2,1)} %bitcast.39, bf16[40,25,4096]{2,0,1:T(8,128)(2,1)} %get-tuple-element.155, bf16[40,25,4096]{2,0,1:T(8,128)(2,1)} %get-tuple-element.154), kind=kOutput, calls=%fused_computation.21 | convolution fusion | flops 6587167744 | bytes 24601760 | tf_op jit(solution)/shard_map/dot_general | solution.py:63
  164.1 0.5 exponential_reduce_fusion
  164.7 0.2 dynamic-update-slice
  164.9 0.2 dynamic-update-slice.1
  165.1 12.2 %all-reduce.2 = (f32[160]{0:T(256)S(1)}, f32[160]{0:T(256)S(1)}) all-reduce(f32[160]{0:T(256)S(1)} %dynamic-update-slice, f32[160]{0:T(256)S(1)} %dynamic-update-slice.1), channel_id=2, replica_groups=mesh['cls'=4,'grp'=4,'dom'=16] {'cls'}, use_global_device_ids=true, to_apply=%add | all-reduce | flops 320 | bytes 2560
  177.3 0.1 reshape.226
  177.4 0.1 reshape.225
  177.5 0.1 while.17
  177.6 0.6 fusion.38
  178.2 0.4 copy.13
  178.6 0.6 reshape.224
  179.1 0.6 copy.14
  179.8 17.3 %fusion.6 = f32[2,200,8192]{2,1,0:T(8,128)} fusion(bf16[2,200,1000]{2,1,0:T(8,128)(2,1)S(1)} %bitcast.41, bf16[1000,4096]{1,0:T(8,128)(2,1)} %mul.222, bf16[1000,4096]{1,0:T(8,128)(2,1)} %mul.221), kind=kOutput, calls=%fused_computation.11 | convolution fusion | flops 6586368000 | bytes 30291200 | tf_op jit(solution)/shard_map/dot_general | solution.py:76
  197.1 0.1 dot_general.34
  197.2 0.1 convolution_bitcast_fusion
  197.4 270.2 %psum.7 = f32[2,8,200]{2,1,0:T(8,128)} all-reduce(f32[2,8,200]{2,1,0:T(8,128)S(1)} %convolution_bitcast_fusion), channel_id=1, replica_groups=mesh['cls'=4,'grp'=4,'dom'=16] {'grp','dom'}, use_global_device_ids=true, to_apply=%region_6.7 | all-reduce | flops 3200 | bytes 25600 | tf_op jit(solution)/shard_map/psum | solution.py:83
  467.6 0.5 add_select_fusion.2
  468.1 31.1 %reduce-scatter.2.cloned.1.call-done = f32[2,200,128]{2,1,0:T(8,128)} async-done(((f32[2,200,8192]{2,1,0:T(8,128)}), f32[2,200,128]{2,1,0:T(8,128)}) %reduce-scatter.2.cloned.1.call-update) | async-done | bytes 204816 | tf_op jit(solution)/shard_map/reduce_scatter | solution.py:80
  (18 shorter events, 0.2 us)
Async XLA Ops:
  7.2 129.5 %all-gather.4.cloned.1.call-start = ((), (), s32[]{:S(2)}) async-start(), calls=%async_computation.1 | async-start | bytes 6656000 | tf_op jit(solution)/shard_map/all_gather | solution.py:59
  7.9 491.3 %reduce-scatter.2.cloned.1.call-start = ((), (), s32[]{:S(2)}) async-start(), calls=%async_computation.2 | async-start | bytes 13312000 | tf_op jit(solution)/shard_map/reduce_scatter | solution.py:80
  55.9 10.3 %copy-start.2 = (u32[256]{0:T(256)S(1)}, u32[256]{0:T(256)}, u32[]{:S(2)}) copy-start(u32[256]{0:T(256)} %constant.111) | copy-start | bytes 3076
  55.9 80.7 %copy-start = (f32[8,4096]{1,0:T(8,128)S(1)}, f32[8,4096]{1,0:T(8,128)}, u32[]{:S(2)}) copy-start(f32[8,4096]{1,0:T(8,128)} %param.10) | copy-start | bytes 393220
  55.9 93.4 %copy-start.1 = (s32[40]{0:T(128)S(1)}, s32[40]{0:T(128)}, u32[]{:S(2)}) copy-start(s32[40]{0:T(128)} %param.8) | copy-start | bytes 484
Sparse Core Ops, SparseCore 0:
  9.8 126.8 all-gather.3
  197.2 301.9 reduce-scatter.1
where the time goes:
time: 512 us; the launch traced here: 506 us
  blocking collectives  282 us (55%)
  waiting for transfers between devices  101 us (20%)
  local copies, waits for them, and re-layouts  47.4 us (9%)
  matrix products  46.3 us (9%)
  between operations  15.5 us (3%)
  other arithmetic  13.4 us (3%)
    psum x1, blocking collectives, body(): class_weights = lax.psum(local_weights, ('grp', 'dom'))  270 us
    all_gather x1, waiting for transfers between devices, body(): piece = lax.all_gather(projections, ('grp', 'dom'), axis=0, tiled=True)  69.2 us
    reduce_scatter x1, waiting for transfers between devices, body(): lax.psum_scatter(sums, ('grp', 'dom'), scatter_dimension=2, tiled=True)  31.1 us
    another operation x2, local copies, waits for them, and re-layouts  24.2 us
    dot_general x1, matrix products, body(): lax.dot_general(low, shifted, (((0,), (0,)), ((), ())), preferred_element...  17.3 us
    dot_general x1, matrix products, body(): scores = jnp.dot(shifted, flat, preferred_element_type=jnp.float32)  14.6 us
    dot_general x1, matrix products, body(): power = jnp.dot(ctf_square, squares, precision=lax.Precision.HIGHEST)  12.6 us
    unnamed x1, blocking collectives  12.2 us
  transfers between devices with their start and end apart: 2, of which 2 were waited for; matrix products, arithmetic and copies ran while one was open for 12% of the time, Pallas kernels for 0%

commit v1 on v0

v1 whole, which is shorter than its diff:
```python
import math

import jax
import jax.numpy as jnp
import numpy as np
from jax import lax
from jax.experimental import pallas as pl
from jax.experimental.pallas import tpu as pltpu
from jax.sharding import Mesh, PartitionSpec as P

IMG = 64
SIDE = 5
SHIFTS = SIDE * SIDE
HALF = SHIFTS // 2
GROUPS = 8
FREQS = IMG * IMG
TWOF = 2 * FREQS
LANE = 128
HIGHEST = lax.Precision.HIGHEST
F32 = jnp.float32
BF16 = jnp.bfloat16
BLOCKS = FREQS // (2 * LANE)
COLS = FREQS // 2


def shift_tables():
    index = np.arange(FREQS)
    shift = np.arange(HALF)
    offx = shift // SIDE - SIDE // 2
    offy = shift % SIDE - SIDE // 2
    phase = (offx[:, None] * (index // IMG)[None, :] + offy[:, None] * (index % IMG)[None, :]) % IMG
    theta = phase.astype(np.float32) * np.float32(2.0 * math.pi / IMG)
    return np.cos(theta.astype(np.float64)).astype(np.float32), np.sin(theta.astype(np.float64)).astype(np.float32)


def build_kernel(core_ref, re_ref, im_ref, hot_ref, ctf_ref, cos_ref, sin_ref, out_ref):
    npart = re_ref.shape[0]
    ctf = jnp.dot(hot_ref[...], ctf_ref[...], precision=HIGHEST, preferred_element_type=F32)
    for g in range(npart // 16):
        rows = slice(16 * g, 16 * g + 16)
        re = ctf[rows] * re_ref[rows, :].astype(F32)
        im = ctf[rows] * im_ref[rows, :].astype(F32)

        def put(s, real, imag):
            at = s * npart + 16 * g
            out_ref[0, 0, at : at + 16, :] = real.astype(BF16)
            out_ref[0, 1, at : at + 16, :] = imag.astype(BF16)

        put(HALF, re, im)
        for s in range(HALF):
            co = cos_ref[s : s + 1, :]
            si = sin_ref[s : s + 1, :]
            a, b, d, e = re * co, im * si, im * co, re * si
            put(s, a + b, d - e)
            put(SHIFTS - 1 - s, a - b, d + e)


def build_shifted(core, images, hot, ctf_table):
    npart = images.shape[0]
    cosv, sinv = shift_tables()

    def place(i, j, core):
        return 2 * j + (core[0] + i) % 2

    grid = pltpu.PrefetchScalarGridSpec(
        num_scalar_prefetch=1,
        grid=(2, BLOCKS),
        in_specs=[
            pl.BlockSpec((npart, LANE), lambda i, j, c: (0, place(i, j, c))),
            pl.BlockSpec((npart, LANE), lambda i, j, c: (0, 2 * BLOCKS + place(i, j, c))),
            pl.BlockSpec((npart, GROUPS), lambda i, j, c: (0, 0)),
            pl.BlockSpec((GROUPS, LANE), lambda i, j, c: (0, place(i, j, c))),
            pl.BlockSpec((HALF, LANE), lambda i, j, c: (0, place(i, j, c))),
            pl.BlockSpec((HALF, LANE), lambda i, j, c: (0, place(i, j, c))),
        ],
        out_specs=pl.BlockSpec((1, 2, npart * SHIFTS, LANE), lambda i, j, c: (i, 0, 0, j)),
    )
    return pl.pallas_call(
        build_kernel,
        grid_spec=grid,
        out_shape=jax.ShapeDtypeStruct((2, 2, npart * SHIFTS, COLS), BF16),
        cost_estimate=pl.CostEstimate(flops=12 * npart * SHIFTS * FREQS, bytes_accessed=4 * npart * SHIFTS * FREQS, transcendentals=0),
        name="build_shifted",
    )(core, images, images, hot, ctf_table, cosv, sinv)


def add_scores(shifted, proj, ctf_ref, acc_ref, power_ref):
    rows = acc_ref.shape[0]
    step = rows // 5
    weights = proj[...]

    for k in range(5):
        at = slice(k * step, k * step + step)
        acc_ref[at, :] += jnp.dot(shifted[0, 0, at, :], weights, preferred_element_type=F32)

    square = weights.astype(F32)
    square = square * square
    high = square.astype(BF16)
    low = (square - high.astype(F32)).astype(BF16)
    left = ctf_ref[0]
    left = left * left
    first = left.astype(BF16)
    rest = left - first.astype(F32)
    second = rest.astype(BF16)
    third = (rest - second.astype(F32)).astype(BF16)
    parts = jnp.concatenate([first.astype(F32), second.astype(F32), third.astype(F32)], axis=0).astype(BF16)
    both = jnp.dot(parts, high, preferred_element_type=F32) + jnp.dot(parts, low, preferred_element_type=F32)
    power_ref[...] += both[:GROUPS] + both[GROUPS : 2 * GROUPS] + both[2 * GROUPS :]


def first_kernel(core_ref, shifted_ref, proj_ref, ctf_ref, acc_ref, power_ref):
    @pl.when((pl.program_id(0) == 0) & (pl.program_id(1) == 0))
    def _():
        acc_ref[...] = jnp.zeros_like(acc_ref)
        power_ref[...] = jnp.zeros_like(power_ref)

    add_scores(shifted_ref, proj_ref, ctf_ref, acc_ref, power_ref)


def second_kernel(core_ref, shifted_ref, proj_ref, ctf_ref, acc0_ref, power0_ref, hot_ref, log_ref, stats_ref, power_ref):
    @pl.when((pl.program_id(0) == 0) & (pl.program_id(1) == 0))
    def _():
        log_ref[...] = acc0_ref[...]
        power_ref[...] = power0_ref[...]

    add_scores(shifted_ref, proj_ref, ctf_ref, log_ref, power_ref)

    @pl.when((pl.program_id(0) == pl.num_programs(0) - 1) & (pl.program_id(1) == pl.num_programs(1) - 1))
    def _():
        npart = hot_ref.shape[0]
        half = 0.5 * jnp.dot(hot_ref[...], power_ref[...], precision=HIGHEST, preferred_element_type=F32)
        best = None
        for s in range(SHIFTS):
            at = slice(s * npart, s * npart + npart)
            value = log_ref[at, :] - half
            log_ref[at, :] = value
            best = value if best is None else jnp.maximum(best, value)
        top = jnp.max(best, axis=1, keepdims=True)
        total = jnp.zeros_like(best)
        for s in range(SHIFTS):
            total = total + jnp.exp(log_ref[s * npart : s * npart + npart, :] - top)
        total = jnp.sum(total, axis=1, keepdims=True)
        lane = lax.broadcasted_iota(jnp.int32, (npart, LANE), 1)
        stats_ref[...] = jnp.where(lane == 0, top, total).T[:8, :]


def score_call(core, shifted, proj, ctf_parts, which, carried=None):
    rows = shifted.shape[2]
    width = proj.shape[1]
    npart = rows // SHIFTS
    depth = 1024
    steps = COLS // depth
    in_specs = [
        pl.BlockSpec((1, 1, rows, depth), lambda i, k, c: (which, i, 0, k)),
        pl.BlockSpec((depth, width), lambda i, k, c: (i * steps + k, 0)),
        pl.BlockSpec((1, GROUPS, depth), lambda i, k, c: ((c[0] + which) % 2, 0, k)),
    ]

    def whole(*shape):
        return pl.BlockSpec(shape, lambda i, k, c: (0,) * len(shape))

    args = [core, shifted, proj, ctf_parts]
    scratch = []
    if carried is None:
        kernel = first_kernel
        out_shape = [jax.ShapeDtypeStruct((rows, width), F32), jax.ShapeDtypeStruct((GROUPS, width), F32)]
        out_specs = [whole(rows, width), whole(GROUPS, width)]
    else:
        kernel = second_kernel
        in_specs += [whole(rows, width), whole(GROUPS, width), whole(npart, GROUPS)]
        args += list(carried)
        out_shape = [jax.ShapeDtypeStruct((rows, width), F32), jax.ShapeDtypeStruct((8, npart), F32)]
        out_specs = [whole(rows, width), whole(8, npart)]
        scratch = [pltpu.VMEM((GROUPS, width), F32)]
    return pl.pallas_call(
        kernel,
        grid_spec=pltpu.PrefetchScalarGridSpec(
            num_scalar_prefetch=1, grid=(2, steps), in_specs=in_specs, out_specs=out_specs, scratch_shapes=scratch
        ),
        out_shape=out_shape,
        cost_estimate=pl.CostEstimate(flops=2 * rows * width * FREQS, bytes_accessed=2 * rows * FREQS, transcendentals=0),
        compiler_params=pltpu.CompilerParams(vmem_limit_bytes=40 * 1024 * 1024),
        name="scores_first" if carried is None else "scores_second",
    )(*args)


def posterior_kernel(log_ref, stats_ref, live_ref, hot_ref, low_ref, weights_ref, evidence_ref, turn_ref):
    npart = hot_ref.shape[1]
    tops = stats_ref[:, 0, :]
    totals = stats_ref[:, 1, :]
    top = jnp.max(tops, axis=0, keepdims=True)
    total = jnp.sum(totals * jnp.exp(tops - top), axis=0, keepdims=True)
    live = live_ref[...]
    evidence_ref[...] = jnp.where(live > 0.0, top + jnp.log(total), 0.0)
    row = lax.broadcasted_iota(jnp.int32, (8, npart), 0)
    turn_ref[...] = jnp.where(row == 0, top, live / total).T
    col_top = turn_ref[:, 0:1]
    scale = turn_ref[:, 1:2]
    gathered = None
    for s in range(SHIFTS):
        at = slice(s * npart, s * npart + npart)
        posterior = jnp.exp(log_ref[at, :] - col_top) * scale
        low_ref[at, :] = posterior.astype(BF16)
        gathered = posterior if gathered is None else gathered + posterior
    weights_ref[...] = jnp.dot(hot_ref[...], gathered, precision=HIGHEST, preferred_element_type=F32)


def posterior_call(loglik, stats, live, hot_t):
    rows, width = loglik.shape
    npart = hot_t.shape[1]
    return pl.pallas_call(
        posterior_kernel,
        out_shape=[
            jax.ShapeDtypeStruct((rows, width), BF16),
            jax.ShapeDtypeStruct((GROUPS, width), F32),
            jax.ShapeDtypeStruct((1, npart), F32),
        ],
        scratch_shapes=[pltpu.VMEM((npart, 8), F32)],
        compiler_params=pltpu.CompilerParams(vmem_limit_bytes=16 * 1024 * 1024),
        name="posterior",
    )(loglik, stats, live, hot_t)


def insert_kernel(low_ref, shifted_ref, out_ref, turn_ref):
    @pl.when((pl.program_id(0) == 0) & (pl.program_id(1) == 0))
    def _():
        turn_ref[...] = low_ref[...].astype(F32).T.astype(BF16)

    sums = jnp.dot(turn_ref[...], shifted_ref[0, 0], preferred_element_type=F32)
    for b in range(out_ref.shape[0]):
        out_ref[b] = sums[:, b * LANE : b * LANE + LANE].astype(out_ref.dtype)


def insert_call(low, shifted, which, dtype):
    rows, width = low.shape
    depth = 512
    steps = COLS // depth
    return pl.pallas_call(
        insert_kernel,
        grid=(2, steps),
        in_specs=[
            pl.BlockSpec((rows, width), lambda i, k: (0, 0)),
            pl.BlockSpec((1, 1, rows, depth), lambda i, k: (which, i, 0, k)),
        ],
        out_specs=pl.BlockSpec((depth // LANE, width, LANE), lambda i, k: (i * steps + k, 0, 0)),
        out_shape=jax.ShapeDtypeStruct((2 * BLOCKS, width, LANE), dtype),
        scratch_shapes=[pltpu.VMEM((width, rows), BF16)],
        cost_estimate=pl.CostEstimate(flops=2 * rows * width * FREQS, bytes_accessed=2 * rows * FREQS, transcendentals=0),
        compiler_params=pltpu.CompilerParams(vmem_limit_bytes=40 * 1024 * 1024),
        name="insert_first" if which else "insert_second",
    )(low, shifted)


CHIPS = ("grp", "y", "zl")
SWAP = [(0, 1), (1, 0)]
SENT = BF16


def body(particle_images, particle_groups, live_counts, ctf_table, projections):
    core = lax.axis_index("core")
    core_arg = core.reshape(1).astype(jnp.int32)
    slots = particle_images.shape[0]
    images = lax.all_gather(particle_images, "core", axis=0, tiled=True)
    groups = lax.all_gather(particle_groups, "core", axis=0, tiled=True)
    counts = lax.all_gather(live_counts, "core", axis=0, tiled=True)
    npart = images.shape[0]
    mine = lax.dynamic_index_in_dim(projections, core, axis=1, keepdims=False)
    theirs = lax.dynamic_index_in_dim(projections, 1 - core, axis=1, keepdims=False)
    given = lax.ppermute(theirs, "core", SWAP)
    proj_own = lax.all_gather(mine, CHIPS, axis=0, tiled=True)
    proj_other = lax.all_gather(given, CHIPS, axis=0, tiled=True)

    group_row = jnp.arange(GROUPS, dtype=jnp.int32)
    hot = (groups[:, None] == group_row[None, :]).astype(F32)
    hot_t = (groups[None, :] == group_row[:, None]).astype(F32)
    slot = jnp.arange(npart, dtype=jnp.int32)
    live = (slot % slots < jnp.repeat(counts, slots)).astype(F32)[None, :]
    ctf_parts = ctf_table.reshape(GROUPS, BLOCKS, 2, LANE).transpose(2, 0, 1, 3).reshape(2, GROUPS, COLS)

    shifted = build_shifted(core_arg, images, hot, ctf_table)
    acc, power = score_call(core_arg, shifted, proj_own, ctf_parts, 0)
    loglik, stats = score_call(core_arg, shifted, proj_other, ctf_parts, 1, (acc, power, hot))
    stats = lax.all_gather(stats[:2], ("cls", "core"), axis=0)
    low, weights, evidence = posterior_call(loglik, stats, live, hot_t)

    sums_other = insert_call(low, shifted, 1, SENT)
    part_other = lax.psum_scatter(sums_other, CHIPS, scatter_dimension=0, tiled=True)
    sums_own = insert_call(low, shifted, 0, SENT)
    part_own = lax.psum_scatter(sums_own, CHIPS, scatter_dimension=0, tiled=True)
    part_other = lax.ppermute(part_other, "core", SWAP)
    own = part_own.reshape(1, -1, LANE).astype(F32)
    other = part_other.reshape(1, -1, LANE).astype(F32)
    insertions = jnp.where(core == 0, jnp.concatenate([own, other]), jnp.concatenate([other, own]))

    weights = lax.psum(weights, CHIPS)
    class_weights = lax.all_gather(weights, "core", axis=0)
    evidence = lax.dynamic_slice_in_dim(evidence[0], core * slots, slots)
    return insertions, class_weights, evidence


def solution(mesh):
    fine = Mesh(mesh.devices.reshape(4, 4, 4, 2, 2), ("cls", "grp", "y", "zl", "core"))
    shards = ("grp", "y", "zl", "core")
    return jax.shard_map(
        body,
        mesh=fine,
        in_specs=(P(shards, None), P(shards), P(shards), P(), P(shards, "cls", None)),
        out_specs=(P("cls", None, shards), P("cls", None, None), P(shards)),
        check_vma=False,
    )
```

time: 512 us -> 731 us (1.43)
  waiting for transfers between devices: 101 us -> 529 us
  blocking collectives: 282 us -> 100 us
  Pallas kernels: 0 us -> 66.7 us
  matrix products: 46.3 us -> 0 us
  local copies, waits for them, and re-layouts: 47.4 us -> 10.6 us
  other arithmetic: 13.4 us -> 2.24 us
    unnamed x2 -> x7, waiting for transfers between devices: 0.7 us -> 234 us
    all_gather x1 -> x3, waiting for transfers between devices: 69.2 us -> 293 us  [the longest x1 149 us: body(): proj_other = lax.all_gather(given, CHIPS, axis=0, tiled=True)]
    psum x1, blocking collectives: 270 us -> 84.7 us  [body(): weights = lax.psum(weights, CHIPS)]
    pallas_call x0 -> x6, Pallas kernels: none -> 66.7 us  [the longest x1 24.9 us: build_shifted(): pl.pallas_call(build_kernel, grid_spec=grid, out_shape=jax.ShapeDtypeStru...]
    dot_general x6 -> x0, matrix products: 46.3 us -> none  [the longest x1 17.3 us: body(): lax.dot_general(low, shifted, (((0,), (0,)), ((), ())), preferred_element...]
    reduce_scatter x1 -> x0, waiting for transfers between devices: 31.1 us -> none  [body(): lax.psum_scatter(sums, ('grp', 'dom'), scatter_dimension=2, tiled=True)]
    another operation x2 -> x0, local copies, waits for them, and re-layouts: 24.2 us -> none
    mul x2 -> x0, local copies, waits for them, and re-layouts: 20.3 us -> none  [the longest x1 10.3 us: build_shifted(): shifted_imag = ctf_rows * (imag * cosv - real * sinv)]
  transfers between devices with their start and end apart: 2 -> 7, of which waited for: 2 -> 6; matrix products, arithmetic and copies ran while one was open for 12% -> 1% of each run, Pallas kernels for 0% -> 6%
where the time goes in v1:
time: 731 us; the launch traced here: 724 us
  waiting for transfers between devices  529 us (72%)
  blocking collectives  100 us (14%)
  Pallas kernels  66.7 us (9%)
  between operations  15.2 us (2%)
  local copies, waits for them, and re-layouts  10.6 us (1%)
    unnamed x7, waiting for transfers between devices  234 us
    all_gather x1, waiting for transfers between devices, body(): proj_other = lax.all_gather(given, CHIPS, axis=0, tiled=True)  149 us
    all_gather x1, waiting for transfers between devices, body(): proj_own = lax.all_gather(mine, CHIPS, axis=0, tiled=True)  136 us
    psum x1, blocking collectives, body(): weights = lax.psum(weights, CHIPS)  84.7 us
    pallas_call x1, Pallas kernels, build_shifted(): pl.pallas_call(build_kernel, grid_spec=grid, out_shape=jax.ShapeDtypeStru...  24.9 us
    pallas_call x2, Pallas kernels, insert_call(): pl.pallas_call(insert_kernel, grid=(2, steps), in_specs=[pl.BlockSpec((ro...  22.5 us
    pallas_call x2, Pallas kernels, score_call(): pl.pallas_call(kernel, grid_spec=pltpu.PrefetchScalarGridSpec(num_scalar_...  18.6 us
  transfers between devices with their start and end apart: 7, of which 6 were waited for; matrix products, arithmetic and copies ran while one was open for 1% of the time, Pallas kernels for 6%

profile of v1, /device:TPU:32, one launch (start us, length us, event | category | flops | bytes accessed | tf_op | source)
XLA Modules:
  0.0 724.2 jit_solution(2472585309755079364)
XLA Ops:
  7.2 0.7 all-gather.7.cloned.1.call-update
  8.0 0.8 constant_dynamic-slice_fusion.1
  8.8 0.7 copy.16
  9.6 0.1 copy.13
  9.8 1.2 collective-permute-done
  11.1 0.6 copy-done.3
  12.4 0.9 copy.18
  13.3 1.3 dynamic-slice.1
  15.3 0.9 dynamic-update-slice
  16.1 0.8 dynamic-update-slice.1
  16.9 1.8 all-reduce.4
  18.9 0.7 fusion.hot_ref
  19.6 7.6 %all-gather.7.cloned.1.call-done.re_ref.im_ref = bf16[80,8192]{1,0:T(8,128)(2,1)} async-done(((bf16[40,8192]{1,0:T(8,128)(2,1)}), bf16[80,8192]{1,0:T(8,128)(2,1)}) %all-gather.7.cloned.1.call-update) | async-done | bytes 1310736 | tf_op jit(solution)/shard_map/all_gather | solution.py:263
  27.2 24.9 %build_shifted.1.shifted_ref = bf16[2,2,2000,2048]{3,2,1,0:T(8,128)(2,1)} custom-call(s32[1]{0:T(128)} %bitcast.core_ref, bf16[80,8192]{1,0:T(8,128)(2,1)} %all-gather.7.cloned.1.call-done.re_ref.im_ref, bf16[80,8192]{1,0:T(8,128)(2,1)} %all-gather.7.cloned.1.call-done.re_ref.im_ref, f32[80,8]{1,0:T(8,128)} %fusion.hot_ref, f32[8,4096]{1,0:T(8,128)} %ctf_ref.1, ...), custom_call_target="tpu_custom_call" | custom-call | flops 98304000 | bytes 32768000 | tf_op jit(solution)/shard_map/build_shifted/pallas_call | solution.py:78
  52.1 136.2 %all-gather.11.cloned.1.call-done = bf16[4096,1,200]{2,0,1:T(8,128)(2,1)} async-done(((bf16[128,1,200]{2,0,1:T(8,128)(2,1)}), bf16[4096,1,200]{2,0,1:T(8,128)(2,1)}) %all-gather.11.cloned.1.call-update) | async-done | bytes 1638416 | tf_op jit(solution)/shard_map/all_gather | solution.py:270
  188.3 1.6 copy-done
  189.9 9.0 %scores_first.1 = (f32[2000,200]{1,0:T(8,128)S(1)}, f32[8,200]{1,0:T(8,128)S(1)}) custom-call(s32[1]{0:T(128)} %bitcast.core_ref, bf16[2,2,2000,2048]{3,2,1,0:T(8,128)(2,1)} %build_shifted.1.shifted_ref, bf16[4096,200]{1,0:T(8,128)(2,1)S(1)} %bitcast.17, f32[2,8,2048]{2,1,0:T(8,128)S(1)} %bitcast.18), custom_call_target="tpu_custom_call" | custom-call | flops 3276800000 | bytes 16384000 | tf_op jit(solution)/shard_map/scores_first/pallas_call | solution.py:175
  198.9 149.2 %all-gather.9.cloned.1.call-done.proj_ref = bf16[4096,200]{1,0:T(8,128)(2,1)} async-done(((bf16[128,200]{1,0:T(8,128)(2,1)}), bf16[4096,200]{1,0:T(8,128)(2,1)}) %all-gather.9.cloned.1.call-update) | async-done | bytes 1638416 | tf_op jit(solution)/shard_map/all_gather | solution.py:271
  348.2 1.6 copy-done.1
  349.8 9.6 %scores_second.1 = (f32[2000,200]{1,0:T(8,128)S(1)}, f32[8,80]{1,0:T(8,128)S(1)}) custom-call(s32[1]{0:T(128)} %bitcast.core_ref, bf16[2,2,2000,2048]{3,2,1,0:T(8,128)(2,1)} %build_shifted.1.shifted_ref, bf16[4096,200]{1,0:T(8,128)(2,1)S(1)} %copy-done.1, f32[2,8,2048]{2,1,0:T(8,128)S(1)} %bitcast.19, f32[2000,200]{1,0:T(8,128)S(1)} %get-tuple-element.10.acc0_ref, ...), custom_call_target="tpu_custom_call" | custom-call | flops 3276800000 | bytes 16384000 | tf_op jit(solution)/shard_map/scores_second/pallas_call | solution.py:175
  359.4 12.1 %all-gather.2.stats_ref = f32[8,2,80]{2,1,0:T(2,128)S(1)} all-gather(f32[1,2,80]{2,1,0:T(2,128)S(1)} %slice_bitcast_fusion), channel_id=3, replica_groups=mesh['cls'=4,'grp'=4,'y'=4,'zl'=2,'core'=2] {'cls','core'}, dimensions={0}, use_global_device_ids=true | all-gather | bytes 5760 | tf_op jit(solution)/shard_map/all_gather | solution.py:283
  371.5 0.7 posterior.1
  372.2 11.2 %insert_first.1 = bf16[32,200,128]{2,1,0:T(8,128)(2,1)} custom-call(bf16[2000,200]{1,0:T(8,128)(2,1)S(1)} %get-tuple-element.14.low_ref, bf16[2,2,2000,2048]{3,2,1,0:T(8,128)(2,1)} %build_shifted.1.shifted_ref), custom_call_target="tpu_custom_call" | custom-call | flops 3276800000 | bytes 16384000 | tf_op jit(solution)/shard_map/insert_first/pallas_call | solution.py:238
  383.5 11.3 %insert_second.1 = bf16[32,200,128]{2,1,0:T(8,128)(2,1)} custom-call(bf16[2000,200]{1,0:T(8,128)(2,1)S(1)} %get-tuple-element.14.low_ref, bf16[2,2,2000,2048]{3,2,1,0:T(8,128)(2,1)} %build_shifted.1.shifted_ref), custom_call_target="tpu_custom_call" | custom-call | flops 3276800000 | bytes 16384000 | tf_op jit(solution)/shard_map/insert_second/pallas_call | solution.py:238
  394.8 151.1 %reduce-scatter.11.cloned.1.call-done = bf16[1,200,128]{2,1,0:T(8,128)(2,1)} async-done(((bf16[32,200,128]{2,1,0:T(8,128)(2,1)}), bf16[1,200,128]{2,1,0:T(8,128)(2,1)}) %reduce-scatter.11.cloned.1.call-update) | async-done | bytes 51216
  545.9 0.6 fusion.2
  546.5 84.7 %psum.7 = f32[1,8,200]{2,1,0:T(8,128)S(1)} all-reduce(f32[1,8,200]{2,1,0:T(8,128)S(1)} %bitcast.20), channel_id=1, replica_groups=mesh['cls'=4,'grp'=4,'y'=4,'zl'=2,'core'=2] {'grp','y','zl'}, use_global_device_ids=true, to_apply=%region_2.3 | all-reduce | flops 1600 | bytes 12800 | tf_op jit(solution)/shard_map/psum | solution.py:295
  631.2 1.8 all_gather.35
  633.0 82.6 %reduce-scatter.9.cloned.1.call-done = bf16[1,200,128]{2,1,0:T(8,128)(2,1)} async-done(((bf16[32,200,128]{2,1,0:T(8,128)(2,1)}), bf16[1,200,128]{2,1,0:T(8,128)(2,1)}) %reduce-scatter.9.cloned.1.call-update) | async-done | bytes 51216
  715.6 0.8 convert_element_type.25
  716.4 0.7 maximum_select_fusion
  717.1 0.6 copy.23
  (25 shorter events, 0.6 us)
Async XLA Ops:
  7.2 20.0 %all-gather.7.cloned.1.call-start = ((), (), s32[]{:S(2)}) async-start(), calls=%async_computation.2 | async-start | bytes 1966080 | tf_op jit(solution)/shard_map/all_gather | solution.py:263
  7.9 180.4 %all-gather.11.cloned.1.call-start = ((), (), s32[]{:S(2)}) async-start(), calls=%async_computation.4 | async-start | bytes 2162688 | tf_op jit(solution)/shard_map/all_gather | solution.py:270
  9.6 338.6 %all-gather.9.cloned.1.call-start = ((), (), s32[]{:S(2)}) async-start(), calls=%async_computation.3 | async-start | bytes 2162688 | tf_op jit(solution)/shard_map/all_gather | solution.py:271
  9.7 1.3 collective-permute-start
  11.1 0.6 copy-start.3
  11.7 534.2 %reduce-scatter.11.cloned.1.call-start = ((), (), s32[]{:S(2)}) async-start(), calls=%async_computation.6 | async-start | bytes 1689600
  188.3 1.6 copy-start
  189.9 158.2 %copy-start.2 = (f32[80,8]{1,0:T(8,128)S(1)}, f32[80,8]{1,0:T(8,128)}, u32[]{:S(2)}) copy-start(f32[80,8]{1,0:T(8,128)} %fusion.hot_ref) | copy-start | bytes 7684
  348.2 1.6 copy-start.1
  383.5 332.1 %reduce-scatter.9.cloned.1.call-start = ((), (), s32[]{:S(2)}) async-start(), calls=%async_computation.5 | async-start | bytes 1689600
  545.9 170.4 %collective-permute-start.1 = (bf16[1,200,128]{2,1,0:T(8,128)(2,1)}, bf16[1,200,128]{2,1,0:T(8,128)(2,1)S(1)}, u32[]{:S(2)}, u32[]{:S(2)}) collective-permute-start(bf16[1,200,128]{2,1,0:T(8,128)(2,1)} %reduce-scatter.11.cloned.1.call-done), channel_id=1, source_target_pairs={{0,1},{1,0},{2,3},{3,2},{4,5},{5,4},{6,7},{7,6},{8,9},{9,8},{10,11... | collective-permute-start | bytes 153608 | tf_op jit(solution)/shard_map/ppermute | solution.py:290
Sparse Core Ops, SparseCore 0:
  9.8 17.3 all-gather.6
  29.0 159.3 all-gather.10
  190.7 157.3 all-gather.8
  383.6 162.3 reduce-scatter.10
  548.5 167.0 reduce-scatter.8
